TPU v7x, 32 devices: a whole 2x2x4 slice. The times are simulated.
32 devices in a mesh: row: 8 (over z, y), col: 4 (over x, core).
Axes of the slice: x: 2, y: 2, z: 4, core: 2. Of those that a mesh axis runs over, the one named last changes fastest.
Arguments:
- roll_embed: bfloat16 [512, 3072], P('col', 'row'), may hold values from -16 to 16
- expert_embed: bfloat16 [512, 8192], P('row', 'col'), may hold values from -16 to 16
- roll_weight: float32 [3072], P('row'), may hold values from 0.5 to 2
- expert_weight: float32 [8192], P('col'), may hold values from 0.5 to 2
Outputs:
- reward: float32 [3072], P('row')
- roll_pull: float32 [512, 3072], P('col', 'row')
- expert_pull: float32 [512, 8192], P('row', 'col')
All inputs are finite; a program needn't handle non-finite values.
Results may differ from a plain program's by a relative error of at most 0.0022.
Values may be sent and summed in bfloat16 or wider, within the bound.
A program may use at most 64 MiB of HBM per device.

v0:
```python
import jax
import jax.numpy as jnp
from jax import lax
from jax.sharding import PartitionSpec as P

ITERS = 3


blur = 0.05


def joined(value, axis, join):
    pieces = jax.tree.map(lambda part: lax.all_gather(part, axis), value)
    head = jax.tree.map(lambda part: part[0], pieces)
    tail = jax.tree.map(lambda part: part[1:], pieces)
    total, _ = lax.scan(lambda total, section: (join(total, section), None), head, tail)
    return total


def combine(first, second):
    high = jnp.maximum(first[0], second[0])
    return (high, first[1] * jnp.exp(first[0] - high) + second[1] * jnp.exp(second[0] - high))


def combine_three(first, second):
    high = jnp.maximum(first[0], second[0])
    lower = jnp.exp(first[0] - high)
    upper = jnp.exp(second[0] - high)
    return (high, first[1] * lower + second[1] * upper, first[2] * lower + second[2] * upper)


def merge_over_col(top, total):
    high = lax.pmax(top, "col")
    summed = lax.psum(total * jnp.exp(top - high), "col")
    return high + jnp.log(summed)


def merge_over_row(top, total):
    high = lax.pmax(top, "row")
    summed = lax.psum(total * jnp.exp(top - high), "row")
    return high + jnp.log(summed)


def shards(roll_embed, expert_embed, roll_weight, expert_weight):
    gathered_x = lax.all_gather(roll_embed, "col", axis=0, tiled=True)
    gathered_y = lax.all_gather(expert_embed, "row", axis=0, tiled=True)
    width = gathered_x.shape[0]
    rows = gathered_x.shape[1]
    cols = gathered_y.shape[1]
    block = min(512, cols)
    count = cols // block
    sqx = jnp.sum(jnp.square(gathered_x.astype(jnp.float32)), 0)
    sqy = jnp.sum(jnp.square(gathered_y.astype(jnp.float32)), 0)
    log_a = blur * jnp.log(roll_weight)
    log_b = blur * jnp.log(expert_weight)
    indices = jnp.arange(count, dtype=jnp.int32)

    def tile(start):
        ycols = lax.dynamic_slice_in_dim(gathered_y, start, block, 1)
        sq_cols = lax.dynamic_slice_in_dim(sqy, start, block, 0)
        cross = lax.dot_general(
            gathered_x, ycols, (((0,), (0,)), ((), ())), preferred_element_type=jnp.float32
        )
        return (sqx[:, None] + sq_cols[None, :] - 2.0 * cross) / width

    def row_pass(gvals):

        def row_step(carry, index):
            start = index * block
            cost = tile(start)
            g_cols = lax.dynamic_slice_in_dim(gvals, start, block, 0)
            score = (g_cols[None, :] - cost) / blur
            top = jnp.max(score, 1)
            total = jnp.sum(jnp.exp(score - top[:, None]), 1)
            return (combine(carry, (top, total)), None)

        init = (jnp.full((rows,), -1e30, jnp.float32), jnp.zeros((rows,), jnp.float32))
        (top, total), _ = lax.scan(row_step, init, indices)
        return merge_over_col(top, total)

    def col_pass(fvals):

        def col_step(carry, index):
            cost = tile(index * block)
            score = (fvals[:, None] - cost) / blur
            top = jnp.max(score, 0)
            total = jnp.sum(jnp.exp(score - top[None, :]), 0)
            return (carry, (top, total))

        _, (top, total) = lax.scan(col_step, 0.0, indices)
        return merge_over_row(top.reshape(cols), total.reshape(cols))

    fvals = jnp.zeros((rows,), jnp.float32)
    gvals = jnp.zeros((cols,), jnp.float32)
    for step_index in range(ITERS):
        fvals = log_a - blur * row_pass(gvals)
        gvals = log_b - blur * col_pass(fvals)

    def final(carry, index):
        start = index * block
        cost = tile(start)
        g_cols = lax.dynamic_slice_in_dim(gvals, start, block, 0)
        score = (g_cols[None, :] - cost) / blur
        top = jnp.max(score, 1)
        shifted = jnp.exp(score - top[:, None])
        local = (top, jnp.sum(shifted, 1), jnp.sum(shifted * cost, 1))
        plan = jnp.exp((fvals[:, None] + g_cols[None, :] - cost) / blur)
        return (combine_three(carry, local), plan.astype(jnp.bfloat16))

    init = (
        jnp.full((rows,), -1e30, jnp.float32),
        jnp.zeros((rows,), jnp.float32),
        jnp.zeros((rows,), jnp.float32),
    )
    (top, shifted_mass, shifted_cost), plan_blocks = lax.scan(final, init, indices)
    high, shifted_mass, shifted_cost = joined(
        (top, shifted_mass, shifted_cost), "col", combine_three
    )
    reward = -shifted_cost / shifted_mass
    rowmass = jnp.exp(fvals / blur + high) * shifted_mass
    y_blocks = gathered_y.reshape(width, count, block)
    pulled = lax.psum_scatter(
        jnp.einsum("fkb,krb->fr", y_blocks, plan_blocks, preferred_element_type=jnp.float32),
        "col",
        scatter_dimension=0,
        tiled=True,
    )
    roll_pull = rowmass[None, :] * roll_embed.astype(jnp.float32) - pulled
    own_rows = expert_embed.shape[0]
    xsum = lax.psum_scatter(
        jnp.einsum(
            "fr,krb->fkb", gathered_x, plan_blocks, preferred_element_type=jnp.float32
        ).reshape(own_rows * lax.axis_size("row"), cols),
        "row",
        scatter_dimension=0,
        tiled=True,
    )
    expert_pull = expert_weight[None, :] * expert_embed.astype(jnp.float32) - xsum
    return (reward, roll_pull, expert_pull)


def solution(mesh):
    placed = (P("col", "row"), P("row", "col"), P("row"), P("col"))
    return jax.shard_map(
        shards,
        mesh=mesh,
        in_specs=placed,
        out_specs=(P("row"), P("col", "row"), P("row", "col")),
        check_vma=False,
    )
```

profile of v0, /device:TPU:0, one launch (start us, length us, event | category | flops | bytes accessed | tf_op | source)
XLA Modules:
  0.0 406.3 jit_solution(18317632272028746261)
XLA Ops:
  7.2 0.7 all-gather.8.cloned.1.call-update
  8.0 8.1 %all_gather.24 = bf16[512,384]{1,0:T(8,128)(2,1)S(1)} all-gather(bf16[128,384]{1,0:T(8,128)(2,1)} %param.20), channel_id=1, replica_groups=mesh['row'=8,'col'=4] {'col'}, dimensions={0}, use_global_device_ids=true | all-gather | bytes 491520 | tf_op jit(solution)/shard_map/all_gather | solution.py:45
  16.3 45.9 %all-gather.8.cloned.1.call-done = bf16[512,2048]{1,0:T(8,128)(2,1)} async-done(((bf16[64,2048]{1,0:T(8,128)(2,1)}), bf16[512,2048]{1,0:T(8,128)(2,1)}) %all-gather.8.cloned.1.call-update) | async-done | bytes 2097168 | tf_op jit(solution)/shard_map/all_gather | solution.py:46
  62.2 2.2 multiply_reduce_fusion.1
  64.4 8.7 %while.110 = (s32[]{:T(128)}, f32[384]{0:T(512)S(1)}, f32[384]{0:T(512)S(1)}, f32[384]{0:T(512)S(1)}, s32[4]{0:T(128)S(1)}, /*index=5*/f32[2048]{0:T(1024)S(1)},...) while((s32[]{:T(128)}, f32[384]{0:T(512)S(1)}, ...), condition=%wide.region_5.6_spmd.clone, body=%wide.region_2.5_spmd.clone.sunk | while | flops 203098368 | bytes 2512585 | solution.py:78
  64.4 0.7 dynamic_slice.167
  66.6 0.7 dynamic_slice.167
  68.7 0.7 dynamic_slice.167
  70.9 0.7 dynamic_slice.167
  73.1 5.7 %pmax.42 = f32[384]{0:T(512)S(1)} all-reduce(f32[384]{0:T(512)S(1)} %get-tuple-element.390), channel_id=1, replica_groups=mesh['row'=8,'col'=4] {'col'}, use_global_device_ids=true, to_apply=%region_6.7 | all-reduce | flops 384 | bytes 3072 | tf_op jit(solution)/shard_map/pmax | solution.py:33
  78.8 6.6 %psum.42 = f32[384]{0:T(512)S(1)} all-reduce(f32[384]{0:T(512)S(1)} %exponential_multiply_fusion.6), channel_id=1, replica_groups=mesh['row'=8,'col'=4] {'col'}, use_global_device_ids=true, to_apply=%region_7.8 | all-reduce | flops 384 | bytes 3072 | tf_op jit(solution)/shard_map/psum | solution.py:34
  85.4 8.9 %while.106 = (s32[]{:T(128)}, f32[4,512]{1,0:T(4,128)S(1)}, f32[4,512]{1,0:T(4,128)S(1)}, f32[384]{0:T(512)S(1)}, f32[384]{0:T(512)S(1)}, /*index=5*/s32[4]{0:T(...) while((s32[]{:T(128)}, f32[4,512]{1,0:T(4,128)S(1)}, ...), condition=%wide.region_11.12_spmd, body=%wide.region_8.11_spmd.sunk | while | flops 203095040 | bytes 2515151 | solution.py:90
  85.4 0.7 dynamic_slice.156
  87.6 0.7 dynamic_slice.156
  89.8 0.7 dynamic_slice.156
  92.1 0.7 dynamic_slice.156
  94.3 19.2 %pmax.43 = f32[2048]{0:T(1024)S(1)} all-reduce(f32[2048]{0:T(1024)S(1)} %bitcast.175), channel_id=1, replica_groups=mesh['row'=8,'col'=4] {'row'}, use_global_device_ids=true, to_apply=%region_12.13 | all-reduce | flops 2048 | bytes 16384 | tf_op jit(solution)/shard_map/pmax | solution.py:39
  113.5 17.6 %psum.43 = f32[2048]{0:T(1024)S(1)} all-reduce(f32[2048]{0:T(1024)S(1)} %exponential_multiply_fusion.2), channel_id=1, replica_groups=mesh['row'=8,'col'=4] {'row'}, use_global_device_ids=true, to_apply=%region_13.14 | all-reduce | flops 2048 | bytes 16384 | tf_op jit(solution)/shard_map/psum | solution.py:40
  131.2 9.0 %while.111 = (s32[]{:T(128)}, f32[384]{0:T(512)S(1)}, f32[384]{0:T(512)S(1)}, s32[4]{0:T(128)S(1)}, f32[2048]{0:T(1024)S(1)}, /*index=5*/f32[384]{0:T(512)S(1)},...) while((s32[]{:T(128)}, f32[384]{0:T(512)S(1)}, ...), condition=%wide.region_17.18_spmd.clone, body=%wide.region_14.17_spmd.clone.sunk | while | flops 203098368 | bytes 2518741 | solution.py:78
  131.2 0.7 dynamic_slice.170
  133.5 0.7 dynamic_slice.170
  135.7 0.7 dynamic_slice.170
  138.0 0.7 dynamic_slice.170
  140.2 5.7 %pmax.44 = f32[384]{0:T(512)S(1)} all-reduce(f32[384]{0:T(512)S(1)} %get-tuple-element.394), channel_id=1, replica_groups=mesh['row'=8,'col'=4] {'col'}, use_global_device_ids=true, to_apply=%region_18.19 | all-reduce | flops 384 | bytes 3072 | tf_op jit(solution)/shard_map/pmax | solution.py:33
  145.9 6.2 %psum.44 = f32[384]{0:T(512)S(1)} all-reduce(f32[384]{0:T(512)S(1)} %exponential_multiply_fusion.5), channel_id=1, replica_groups=mesh['row'=8,'col'=4] {'col'}, use_global_device_ids=true, to_apply=%region_19.20 | all-reduce | flops 384 | bytes 3072 | tf_op jit(solution)/shard_map/psum | solution.py:34
  152.2 8.9 %while.107 = (s32[]{:T(128)}, f32[4,512]{1,0:T(4,128)S(1)}, f32[4,512]{1,0:T(4,128)S(1)}, f32[384]{0:T(512)S(1)}, f32[384]{0:T(512)S(1)}, /*index=5*/s32[4]{0:T(...) while((s32[]{:T(128)}, f32[4,512]{1,0:T(4,128)S(1)}, ...), condition=%wide.region_23.24_spmd, body=%wide.region_20.23_spmd.sunk | while | flops 203095040 | bytes 2515151 | solution.py:90
  152.2 0.7 dynamic_slice.159
  154.4 0.7 dynamic_slice.159
  156.6 0.7 dynamic_slice.159
  158.8 0.7 dynamic_slice.159
  161.0 19.1 %pmax.45 = f32[2048]{0:T(1024)S(1)} all-reduce(f32[2048]{0:T(1024)S(1)} %bitcast.177), channel_id=1, replica_groups=mesh['row'=8,'col'=4] {'row'}, use_global_device_ids=true, to_apply=%region_24.25 | all-reduce | flops 2048 | bytes 16384 | tf_op jit(solution)/shard_map/pmax | solution.py:39
  180.1 17.9 %psum.45 = f32[2048]{0:T(1024)S(1)} all-reduce(f32[2048]{0:T(1024)S(1)} %exponential_multiply_fusion.1), channel_id=1, replica_groups=mesh['row'=8,'col'=4] {'row'}, use_global_device_ids=true, to_apply=%region_25.26 | all-reduce | flops 2048 | bytes 16384 | tf_op jit(solution)/shard_map/psum | solution.py:40
  198.1 9.0 %while.112 = (s32[]{:T(128)}, f32[384]{0:T(512)S(1)}, f32[384]{0:T(512)S(1)}, s32[4]{0:T(128)S(1)}, f32[2048]{0:T(1024)S(1)}, /*index=5*/f32[384]{0:T(512)S(1)},...) while((s32[]{:T(128)}, f32[384]{0:T(512)S(1)}, ...), condition=%wide.region_29.30_spmd.clone, body=%wide.region_26.29_spmd.clone.sunk | while | flops 203098368 | bytes 2518741 | solution.py:78
  198.1 0.7 dynamic_slice.174
  200.3 0.7 dynamic_slice.174
  202.6 0.7 dynamic_slice.174
  204.8 0.7 dynamic_slice.174
  207.1 5.7 %pmax.46 = f32[384]{0:T(512)S(1)} all-reduce(f32[384]{0:T(512)S(1)} %get-tuple-element.398), channel_id=1, replica_groups=mesh['row'=8,'col'=4] {'col'}, use_global_device_ids=true, to_apply=%region_30.31 | all-reduce | flops 384 | bytes 3072 | tf_op jit(solution)/shard_map/pmax | solution.py:33
  212.7 6.4 %psum.46 = f32[384]{0:T(512)S(1)} all-reduce(f32[384]{0:T(512)S(1)} %exponential_multiply_fusion.4), channel_id=1, replica_groups=mesh['row'=8,'col'=4] {'col'}, use_global_device_ids=true, to_apply=%region_31.32 | all-reduce | flops 384 | bytes 3072 | tf_op jit(solution)/shard_map/psum | solution.py:34
  219.2 8.9 %while.108 = (s32[]{:T(128)}, f32[4,512]{1,0:T(4,128)S(1)}, f32[4,512]{1,0:T(4,128)S(1)}, f32[384]{0:T(512)S(1)}, f32[384]{0:T(512)S(1)}, /*index=5*/s32[4]{0:T(...) while((s32[]{:T(128)}, f32[4,512]{1,0:T(4,128)S(1)}, ...), condition=%wide.region_35.36_spmd, body=%wide.region_32.35_spmd.sunk | while | flops 203095040 | bytes 2515151 | solution.py:90
  219.2 0.7 dynamic_slice.162
  221.4 0.7 dynamic_slice.162
  223.6 0.7 dynamic_slice.162
  225.8 0.7 dynamic_slice.162
  228.1 19.0 %pmax.47 = f32[2048]{0:T(1024)S(1)} all-reduce(f32[2048]{0:T(1024)S(1)} %bitcast.179), channel_id=1, replica_groups=mesh['row'=8,'col'=4] {'row'}, use_global_device_ids=true, to_apply=%region_36.37 | all-reduce | flops 2048 | bytes 16384 | tf_op jit(solution)/shard_map/pmax | solution.py:39
  247.2 17.7 %psum.47 = f32[2048]{0:T(1024)S(1)} all-reduce(f32[2048]{0:T(1024)S(1)} %exponential_multiply_fusion), channel_id=1, replica_groups=mesh['row'=8,'col'=4] {'row'}, use_global_device_ids=true, to_apply=%region_37.38 | all-reduce | flops 2048 | bytes 16384 | tf_op jit(solution)/shard_map/psum | solution.py:40
  264.9 13.0 %while.113 = (s32[]{:T(128)}, f32[384]{0:T(512)S(1)}, f32[384]{0:T(512)S(1)}, f32[384]{0:T(512)S(1)}, bf16[4,384,512]{1,2,0:T(8,128)(2,1)}, /*index=5*/s32[4]{0:...) while((s32[]{:T(128)}, f32[384]{0:T(512)S(1)}, ...), condition=%wide.region_42.43_spmd.clone, body=%wide.region_38.42_spmd.clone.sunk | while | flops 204673536 | bytes 3717874 | solution.py:115
  267.2 1.0 fusion.113
  270.5 1.0 fusion.113
  273.7 1.0 fusion.113
  277.0 1.0 fusion.113
  277.9 2.5 copy.25
  280.4 4.1 %convolution_bitcast_fusion = f32[512,384]{0,1:T(8,128)} fusion(bf16[4,384,512]{1,2,0:T(8,128)(2,1)} %get-tuple-element.408, bf16[512,4,512]{0,2,1:T(8,128)(2,1)} %bitcast.168), kind=kOutput, calls=%fused_computation.92 | convolution fusion | flops 805306368 | bytes 4456448 | tf_op jit(solution)/shard_map/fkb,krb->fr/dot_general | solution.py:123
  284.7 3.3 fusion.56
  287.9 5.4 %copy.28 = f32[512,2048]{1,0:T(8,128)} copy(f32[512,2048]{0,1:T(8,128)} %bitcast.167) | data formatting | bytes 8388608 | tf_op jit(solution)/shard_map/reshape | solution.py:133
  293.4 0.9 copy-done.3
  294.4 5.2 %all-gather.5 = f32[4,1,384]{2,1,0:T(1,128)S(1)} all-gather(f32[1,1,384]{2,1,0:T(1,128)S(1)} %reshape.98), channel_id=4, replica_groups=mesh['row'=8,'col'=4] {'col'}, dimensions={0}, use_global_device_ids=true | all-gather | bytes 7680 | tf_op jit(solution)/shard_map/all_gather | solution.py:13
  299.5 5.1 %all-gather.4 = f32[4,1,384]{2,1,0:T(1,128)S(1)} all-gather(f32[1,1,384]{2,1,0:T(1,128)S(1)} %reshape.96), channel_id=3, replica_groups=mesh['row'=8,'col'=4] {'col'}, dimensions={0}, use_global_device_ids=true | all-gather | bytes 7680 | tf_op jit(solution)/shard_map/all_gather | solution.py:13
  304.7 5.1 %all-gather.3 = f32[4,1,384]{2,1,0:T(1,128)S(1)} all-gather(f32[1,1,384]{2,1,0:T(1,128)S(1)} %reshape.94), channel_id=2, replica_groups=mesh['row'=8,'col'=4] {'col'}, dimensions={0}, use_global_device_ids=true | all-gather | bytes 7680 | tf_op jit(solution)/shard_map/all_gather | solution.py:13
  310.2 0.6 exponential_multiply_fusion.3
  310.8 1.0 multiply_subtract_fusion.1
  311.9 0.8 copy.29
  312.7 85.2 %reduce-scatter.5.cloned.1.call-done = f32[64,2048]{1,0:T(8,128)} async-done(((f32[512,2048]{1,0:T(8,128)}), f32[64,2048]{1,0:T(8,128)}) %reduce-scatter.5.cloned.1.call-update) | async-done | bytes 524304 | tf_op jit(solution)/shard_map/reduce_scatter | solution.py:130
  397.9 1.9 multiply_subtract_fusion
  (236 shorter events, 27.7 us)
Async XLA Ops:
  7.2 55.0 %all-gather.8.cloned.1.call-start = ((), (), s32[]{:S(2)}) async-start(), calls=%async_computation.2 | async-start | bytes 2359296 | tf_op jit(solution)/shard_map/all_gather | solution.py:46
  7.9 302.9 %reduce-scatter.3.cloned.1.call-start = ((), (), s32[]{:S(2)}) async-start(), calls=%async_computation.3 | async-start | bytes 983040 | tf_op jit(solution)/shard_map/reduce_scatter | solution.py:122
  62.2 2.2 copy-start
  64.4 21.0 %copy-start.5 = (f32[384]{0:T(512)S(1)}, f32[384]{0:T(512)}, u32[]{:S(2)}) copy-start(f32[384]{0:T(512)} %param.22) | copy-start | bytes 4612
  85.4 45.8 %copy-start.4 = (f32[2048]{0:T(1024)S(1)}, f32[2048]{0:T(1024)}, u32[]{:S(2)}) copy-start(f32[2048]{0:T(1024)} %param.23) | copy-start | bytes 24580
  280.4 4.2 %copy-start.1 = (bf16[4,384,512]{1,2,0:T(8,128)(2,1)S(1)}, bf16[4,384,512]{1,2,0:T(8,128)(2,1)}, u32[]{:S(2)}) copy-start(bf16[4,384,512]{1,2,0:T(8,128)(2,1)} %get-tuple-element.408) | copy-start | bytes 4718596
  284.6 113.3 %reduce-scatter.5.cloned.1.call-start = ((), (), s32[]{:S(2)}) async-start(), calls=%async_computation.4 | async-start | bytes 4718592 | tf_op jit(solution)/shard_map/reduce_scatter | solution.py:130
  293.3 0.9 copy-start.3
  293.3 104.6 %copy-start.2 = (bf16[64,2048]{1,0:T(8,128)(2,1)S(1)}, bf16[64,2048]{1,0:T(8,128)(2,1)}, u32[]{:S(2)}) copy-start(bf16[64,2048]{1,0:T(8,128)(2,1)} %param.21) | copy-start | bytes 786436
Sparse Core Ops, SparseCore 0:
  10.1 51.9 all-gather.7
  284.7 20.9 reduce-scatter.2
  309.8 88.0 reduce-scatter.4
where the time goes:
time: 407 us; the launch traced here: 406 us
  blocking collectives  170 us (42%)
  waiting for transfers between devices  132 us (32%)
  local copies, waits for them, and re-layouts  32.6 us (8%)
  matrix products  21.9 us (5%)
  loops' own time  20.1 us (5%)
  other arithmetic  15.3 us (4%)
  between operations  14.2 us (3%)
    reduce_scatter x1, waiting for transfers between devices, shards(): lax.psum_scatter(jnp.einsum('fr,krb->fkb', gathered_x, plan_blocks, prefe...  85.2 us
    pmax x3, blocking collectives, merge_over_row(): high = lax.pmax(top, 'row')  57.3 us
    psum x3, blocking collectives, merge_over_row(): summed = lax.psum(total * jnp.exp(top - high), 'row')  53.2 us
    all_gather x1, waiting for transfers between devices, shards(): gathered_y = lax.all_gather(expert_embed, 'row', axis=0, tiled=True)  45.9 us
    psum x3, blocking collectives, merge_over_col(): summed = lax.psum(total * jnp.exp(top - high), 'col')  19.2 us
    dynamic_slice x28, local copies, waits for them, and re-layouts, row_pass(): (top, total), _ = lax.scan(row_step, init, indices)  18.3 us
    pmax x3, blocking collectives, merge_over_col(): high = lax.pmax(top, 'col')  17 us
    all_gather x3, blocking collectives, joined(): pieces = jax.tree.map(lambda part: lax.all_gather(part, axis), value)  15.4 us
  transfers between devices with their start and end apart: 3, of which 2 were waited for; matrix products, arithmetic and copies ran while one was open for 3% of the time, Pallas kernels for 0%

commit v1 on v0

v1 whole, which is shorter than its diff:
```python
import functools
import math

import jax
import jax.numpy as jnp
from jax import lax
from jax.experimental import pallas as pl
from jax.experimental.pallas import tpu as pltpu
from jax.sharding import PartitionSpec as P

ITERS = 3


blur = 0.05

LANES = 128
LOG2E = math.log2(math.e)
MESH = pl.DeviceIdType.MESH


def lse2(parts):
    top = jnp.max(parts, 0)
    return top + jnp.log(jnp.sum(jnp.exp2(parts - top[None]), 0)) * LOG2E


def tile_rows(blocks):
    return -(-blocks // 8) * 8


def kernel(
    zn, yn, cn, x_ref, y_ref, a_ref, b_ref,
    reward_ref, mass_ref, pulled_ref, xsum_ref,
    xg, yg, neg, plan, fbc, logw, fslots, gslots, rslots, fv, gv,
    xsend, xrecv, psend, precv,
    local_sem, xs, xr, ys, yr, ws, wr, fs, fr, gs, gr, rs, rr, us, ur, ps, pr,
):
    row, col = lax.axis_index("row"), lax.axis_index("col")
    z, y = lax.div(row, yn), lax.rem(row, yn)
    nrow, ncube = zn * yn, cn * yn
    q = col * yn + y
    fx, own_rows = x_ref.shape
    fy = y_ref.shape[0]
    width, rows = xg.shape
    cols = yg.shape[1]
    rblocks, cblocks = rows // LANES, cols // LANES

    def cube_device(index):
        return (z * yn + lax.rem(index, yn), lax.div(index, yn))

    def each(count, body):
        def step(i, carry):
            body(i)
            return carry
        lax.fori_loop(0, count, step, 0)

    def others(count, me, body):
        each(count - 1, lambda i: body(lax.rem(me + i + 1, count)))

    def band(index, size):
        return pl.ds(pl.multiple_of(index * size, size), size)

    fslots[...] = jnp.zeros(fslots.shape, jnp.float32)
    gslots[...] = jnp.zeros(gslots.shape, jnp.float32)
    rslots[...] = jnp.zeros(rslots.shape, jnp.float32)
    barrier = pltpu.get_barrier_semaphore()
    others(nrow, row, lambda r: pl.semaphore_signal(
        barrier, inc=1, device_id=(r, col), device_id_type=MESH))
    others(ncube, q, lambda p: pl.semaphore_signal(
        barrier, inc=1, device_id=cube_device(p), device_id_type=MESH))
    pl.semaphore_wait(barrier, nrow - 1 + ncube - 1)

    def y_copy(dest, origin):
        return pltpu.make_async_remote_copy(
            src_ref=y_ref.at[:, band(lax.rem(dest, yn), cols)],
            dst_ref=yg.at[band(origin, fy), :],
            send_sem=ys.at[dest], recv_sem=yr.at[origin],
            device_id=(dest, col), device_id_type=MESH)

    def x_copy(dest, origin):
        return pltpu.make_async_remote_copy(
            src_ref=x_ref,
            dst_ref=xg.at[band(lax.div(origin, yn), fx), band(lax.rem(origin, yn), own_rows)],
            send_sem=xs.at[dest], recv_sem=xr.at[origin],
            device_id=cube_device(dest), device_id_type=MESH)

    def w_copy(dest, origin):
        return pltpu.make_async_remote_copy(
            src_ref=logw.at[origin], dst_ref=logw.at[origin],
            send_sem=ws.at[dest], recv_sem=wr.at[origin],
            device_id=(z * yn + dest, col), device_id_type=MESH)

    others(nrow, row, lambda r: y_copy(r, row).start())
    others(ncube, q, lambda p: x_copy(p, q).start())
    own_blocks = own_rows // LANES
    logw[y] = jnp.zeros(logw.shape[1:], jnp.float32)
    logw[y, 0:own_blocks, :] = jnp.log(a_ref[...]) * LOG2E
    others(yn, y, lambda p: w_copy(p, y).start())
    own_y = pltpu.make_async_copy(
        y_ref.at[:, band(y, cols)], yg.at[band(row, fy), :], local_sem.at[0])
    own_x = pltpu.make_async_copy(
        x_ref, xg.at[band(col, fx), band(y, own_rows)], local_sem.at[1])
    own_y.start()
    own_x.start()
    fv[...] = jnp.zeros(fv.shape, jnp.float32)
    gv[...] = jnp.zeros(gv.shape, jnp.float32)
    log_b = jnp.log(b_ref[y]) * LOG2E
    own_y.wait()
    own_x.wait()
    others(yn, y, lambda p: w_copy(p, p).wait_recv())
    others(ncube, q, lambda p: x_copy(p, p).wait_recv())

    def spread(line):
        return jnp.transpose(jnp.broadcast_to(line, (LANES, LANES)))

    def gather_line(column):
        return jnp.transpose(jnp.broadcast_to(column, (LANES, LANES)))[0:1, :]

    log_a = jnp.concatenate([logw[p, 0:own_blocks, :] for p in range(yn)], 0)
    others(nrow, row, lambda r: y_copy(r, r).wait_recv())

    scale = LOG2E / (blur * width)
    yall = yg[...].astype(jnp.float32)
    sqy = jnp.sum(yall * yall, 0, keepdims=True)

    def cost_block(i):
        xb = xg[:, band(i, LANES)]
        xf = xb.astype(jnp.float32)
        sqx = spread(jnp.sum(xf * xf, 0, keepdims=True))[:, 0:1]
        cross = lax.dot_general(
            xb, yg[...], (((0,), (0,)), ((), ())), preferred_element_type=jnp.float32)
        neg[band(i, LANES), :] = (2.0 * cross - (sqx + sqy)) * scale
    each(rblocks, cost_block)

    def row_block(i):
        here = band(i, LANES)

        def score(k):
            return neg[here, k * LANES:(k + 1) * LANES] + gv[k:k + 1, :]

        high = score(0)
        for k in range(1, cblocks):
            high = jnp.maximum(high, score(k))
        top = jnp.max(high, 1, keepdims=True)
        return here, score, top

    def finish(top, total):
        return top + jnp.log(jnp.sum(total, 1, keepdims=True)) * LOG2E

    def exchange(slots, count, me, sends, recvs, device):
        def copy(dest, origin):
            return pltpu.make_async_remote_copy(
                src_ref=slots.at[origin], dst_ref=slots.at[origin],
                send_sem=sends.at[dest], recv_sem=recvs.at[origin],
                device_id=device(dest), device_id_type=MESH)
        others(count, me, lambda p: copy(p, me).start())

        def arrive():
            others(count, me, lambda p: copy(p, p).wait_recv())

        def leave():
            others(count, me, lambda p: copy(p, me).wait_send())
        return arrive, leave

    leaves = []
    for t in range(ITERS):
        def row_pass(i):
            here, score, top = row_block(i)
            total = jnp.exp2(score(0) - top)
            for k in range(1, cblocks):
                total = total + jnp.exp2(score(k) - top)
            fslots[t, q, pl.ds(i, 1), :] = gather_line(finish(top, total))
        each(rblocks, row_pass)
        arrive, leave = exchange(fslots.at[t], ncube, q, fs.at[t], fr.at[t], cube_device)
        leaves.append(leave)
        arrive()
        fv[0:rblocks, :] = log_a - lse2(fslots[t, :, 0:rblocks, :])
        for i in range(rblocks):
            fbc[i * LANES:(i + 1) * LANES, :] = spread(fv[i:i + 1, :])

        def col_pass(k):
            here = band(k, LANES)

            def score(i):
                part = slice(i * LANES, (i + 1) * LANES)
                return neg[part, here] + fbc[part, :]

            high = score(0)
            for i in range(1, rblocks):
                high = jnp.maximum(high, score(i))
            top = jnp.max(high, 0, keepdims=True)
            total = jnp.exp2(score(0) - top)
            for i in range(1, rblocks):
                total = total + jnp.exp2(score(i) - top)
            line = top + jnp.log(jnp.sum(total, 0, keepdims=True)) * LOG2E
            gslots[t, z, pl.ds(k, 1), :] = line
        each(cblocks, col_pass)
        arrive, leave = exchange(
            gslots.at[t], zn, z, gs.at[t], gr.at[t], lambda p: (p * yn + y, col))
        leaves.append(leave)
        arrive()
        gv[0:cblocks, :] = log_b - lse2(gslots[t, :, 0:cblocks, :])

    def plan_block(i):
        here = band(i, LANES)
        for k in range(cblocks):
            part = slice(k * LANES, (k + 1) * LANES)
            value = jnp.exp2(neg[here, part] + fbc[here, :] + gv[k:k + 1, :])
            plan[here, part] = value.astype(jnp.bfloat16)
    each(rblocks, plan_block)

    step = 2 * LANES if cols % (2 * LANES) == 0 else LANES

    def xsum_block(k):
        here = band(k, step)
        xsend[:, here] = jnp.dot(
            xg[...], plan[:, here], preferred_element_type=jnp.float32).astype(jnp.bfloat16)
    each(cols // step, xsum_block)

    def u_copy(dest, origin):
        return pltpu.make_async_remote_copy(
            src_ref=xsend.at[band(dest, fy), :], dst_ref=xrecv.at[origin],
            send_sem=us.at[dest], recv_sem=ur.at[origin],
            device_id=(dest, col), device_id_type=MESH)
    others(nrow, row, lambda r: u_copy(r, row).start())
    own_u = pltpu.make_async_copy(xsend.at[band(row, fy), :], xrecv.at[row], local_sem.at[0])
    own_u.start()

    rstep = 2 * LANES if rows % (2 * LANES) == 0 else LANES

    def pull_block(i):
        here = band(i, rstep)
        psend[:, here] = lax.dot_general(
            yg[...], plan[here, :], (((1,), (1,)), ((), ())),
            preferred_element_type=jnp.float32).astype(jnp.bfloat16)
    each(rows // rstep, pull_block)

    def p_source(dest):
        return psend.at[band(lax.div(dest, yn), fx), band(lax.rem(dest, yn), own_rows)]

    def p_copy(dest, origin):
        return pltpu.make_async_remote_copy(
            src_ref=p_source(dest), dst_ref=precv.at[origin],
            send_sem=ps.at[dest], recv_sem=pr.at[origin],
            device_id=cube_device(dest), device_id_type=MESH)
    others(ncube, q, lambda p: p_copy(p, q).start())
    own_p = pltpu.make_async_copy(p_source(q), precv.at[q], local_sem.at[1])
    own_p.start()

    half = rslots.shape[1] // 2

    def reward_pass(i):
        here, score, top = row_block(i)
        total = jnp.zeros((LANES, LANES), jnp.float32)
        moment = jnp.zeros((LANES, LANES), jnp.float32)
        for k in range(cblocks):
            weight = jnp.exp2(score(k) - top)
            total = total + weight
            moment = moment + weight * neg[here, k * LANES:(k + 1) * LANES]
        mean = jnp.sum(moment, 1, keepdims=True) / jnp.sum(total, 1, keepdims=True)
        rslots[q, pl.ds(i, 1), :] = gather_line(finish(top, total))
        rslots[q, pl.ds(half + i, 1), :] = gather_line(mean)
    each(rblocks, reward_pass)
    arrive, leave = exchange(rslots, ncube, q, rs, rr, cube_device)
    leaves.append(leave)
    arrive()
    logs = rslots[:, 0:rblocks, :]
    top = jnp.max(logs, 0)
    share = jnp.exp2(logs - top[None])
    total = jnp.sum(share, 0)
    mean = jnp.sum(share * rslots[:, half:half + rblocks, :], 0) / total
    reward_ref[...] = mean * (blur / LOG2E)
    mass_ref[...] = jnp.exp2(fv[0:rblocks, :] + top) * total

    own_p.wait()
    others(ncube, q, lambda p: p_copy(p, p).wait_recv())
    summed = precv[0].astype(jnp.float32)
    for p in range(1, ncube):
        summed = summed + precv[p].astype(jnp.float32)
    pulled_ref[...] = summed
    own_u.wait()
    others(nrow, row, lambda r: u_copy(r, r).wait_recv())
    for p in range(yn):
        summed = xrecv[p].astype(jnp.float32)
        for s in range(1, zn):
            summed = summed + xrecv[s * yn + p].astype(jnp.float32)
        xsum_ref[:, p * cols:(p + 1) * cols] = summed

    others(nrow, row, lambda r: y_copy(r, row).wait_send())
    others(ncube, q, lambda p: x_copy(p, q).wait_send())
    others(yn, y, lambda p: w_copy(p, y).wait_send())
    for leave in leaves:
        leave()
    others(nrow, row, lambda r: u_copy(r, row).wait_send())
    others(ncube, q, lambda p: p_copy(p, q).wait_send())


def shards(zn, yn, cn, roll_embed, expert_embed, roll_weight, expert_weight):
    fx, own_rows = roll_embed.shape
    fy, own_cols = expert_embed.shape
    width = fx * cn
    rows, cols = own_rows * yn, own_cols // yn
    rblocks, cblocks = rows // LANES, cols // LANES
    nrow, ncube = zn * yn, cn * yn
    f32, bf16 = jnp.float32, jnp.bfloat16
    dma = pltpu.SemaphoreType.DMA
    rt, ct, wt = tile_rows(rblocks), tile_rows(cblocks), tile_rows(own_rows // LANES)
    vmem = pl.BlockSpec(memory_space=pltpu.VMEM)
    reward, mass, pulled, xsum = pl.pallas_call(
        functools.partial(kernel, zn, yn, cn),
        out_shape=(
            jax.ShapeDtypeStruct((rblocks, LANES), f32),
            jax.ShapeDtypeStruct((rblocks, LANES), f32),
            jax.ShapeDtypeStruct((fx, own_rows), f32),
            jax.ShapeDtypeStruct((fy, own_cols), f32),
        ),
        in_specs=[vmem] * 4,
        out_specs=[vmem] * 4,
        scratch_shapes=[
            pltpu.VMEM((width, rows), bf16),
            pltpu.VMEM((width, cols), bf16),
            pltpu.VMEM((rows, cols), f32),
            pltpu.VMEM((rows, cols), bf16),
            pltpu.VMEM((rows, LANES), f32),
            pltpu.VMEM((yn, wt, LANES), f32),
            pltpu.VMEM((ITERS, ncube, rt, LANES), f32),
            pltpu.VMEM((ITERS, zn, ct, LANES), f32),
            pltpu.VMEM((ncube, 2 * rt, LANES), f32),
            pltpu.VMEM((rt, LANES), f32),
            pltpu.VMEM((ct, LANES), f32),
            pltpu.VMEM((width, cols), bf16),
            pltpu.VMEM((nrow, fy, cols), bf16),
            pltpu.VMEM((width, rows), bf16),
            pltpu.VMEM((ncube, fx, own_rows), bf16),
            dma((2,)),
            dma((ncube,)), dma((ncube,)),
            dma((nrow,)), dma((nrow,)),
            dma((yn,)), dma((yn,)),
            dma((ITERS, ncube)), dma((ITERS, ncube)),
            dma((ITERS, zn)), dma((ITERS, zn)),
            dma((ncube,)), dma((ncube,)),
            dma((nrow,)), dma((nrow,)),
            dma((ncube,)), dma((ncube,)),
        ],
        compiler_params=pltpu.CompilerParams(
            collective_id=0, has_side_effects=True, vmem_limit_bytes=40 * 2**20),
        cost_estimate=pl.CostEstimate(
            flops=6 * rows * cols * width, bytes_accessed=4 * fy * own_cols,
            transcendentals=8 * rows * cols),
    )(
        roll_embed, expert_embed,
        roll_weight.reshape(own_rows // LANES, LANES),
        expert_weight.reshape(yn, cblocks, LANES),
    )
    start = lax.rem(lax.axis_index("row"), yn) * own_rows
    reward = lax.dynamic_slice_in_dim(reward.reshape(rows), start, own_rows, 0)
    mass = lax.dynamic_slice_in_dim(mass.reshape(rows), start, own_rows, 0)
    roll_pull = mass[None, :] * roll_embed.astype(f32) - pulled
    expert_pull = expert_weight[None, :] * expert_embed.astype(f32) - xsum
    return (reward, roll_pull, expert_pull)


def solution(mesh):
    cn = mesh.shape["col"]
    yn = max(cn // 2, 1)
    if mesh.shape["row"] % yn:
        yn = 1
    zn = mesh.shape["row"] // yn
    placed = (P("col", "row"), P("row", "col"), P("row"), P("col"))
    return jax.shard_map(
        functools.partial(shards, zn, yn, cn),
        mesh=mesh,
        in_specs=placed,
        out_specs=(P("row"), P("col", "row"), P("row", "col")),
        check_vma=False,
    )
```

time: 407 us -> 94.1 us (0.23)
  blocking collectives: 170 us -> 0 us
  waiting for transfers between devices: 132 us -> 0 us
  Pallas kernels: 0 us -> 88.4 us
  local copies, waits for them, and re-layouts: 32.6 us -> 3.25 us
  matrix products: 21.9 us -> 0 us
  loops' own time: 20.1 us -> 0 us
  other arithmetic: 15.3 us -> 1.57 us
  between operations: 14.2 us -> 0.67 us
    pallas_call x0 -> x1, Pallas kernels: none -> 88.4 us  [shards(): pl.pallas_call(functools.partial(kernel, zn, yn, cn), out_shape=(jax.Shap...]
    reduce_scatter x2 -> x0, waiting for transfers between devices: 85.2 us -> none  [the longest x1 85.2 us: shards(): lax.psum_scatter(jnp.einsum('fr,krb->fkb', gathered_x, plan_blocks, prefe...]
    pmax x6 -> x0, blocking collectives: 74.3 us -> none  [the longest x3 57.3 us: merge_over_row(): high = lax.pmax(top, 'row')]
    psum x6 -> x0, blocking collectives: 72.5 us -> none  [the longest x3 53.2 us: merge_over_row(): summed = lax.psum(total * jnp.exp(top - high), 'row')]
    all_gather x1 -> x0, waiting for transfers between devices: 45.9 us -> none  [shards(): gathered_y = lax.all_gather(expert_embed, 'row', axis=0, tiled=True)]
    all_gather x4 -> x0, blocking collectives: 23.6 us -> none  [the longest x3 15.4 us: joined(): pieces = jax.tree.map(lambda part: lax.all_gather(part, axis), value)]
    dot_general x30 -> x0, matrix products: 21.9 us -> none  [the longest x28 14.5 us: tile(): lax.dot_general(gathered_x, ycols, (((0,), (0,)), ((), ())), preferred_el...]
    dynamic_slice x74 -> x2, local copies, waits for them, and re-layouts: 21.6 us -> 0.73 us  [the longest x1 0.66 us: shards(): reward = lax.dynamic_slice_in_dim(reward.reshape(rows), start, own_rows, 0)]
  transfers between devices with their start and end apart: 3 -> 0, of which waited for: 2 -> 0; matrix products, arithmetic and copies ran while one was open for 3% -> 0% of each run, Pallas kernels for 0% -> 0%
where the time goes in v1:
time: 94.1 us; the launch traced here: 93.9 us
  Pallas kernels  88.4 us (94%)
  local copies, waits for them, and re-layouts  3.25 us (3%)
  other arithmetic  1.57 us (2%)
    pallas_call x1, Pallas kernels, shards(): pl.pallas_call(functools.partial(kernel, zn, yn, cn), out_shape=(jax.Shap...  88.4 us
    unnamed x8, local copies, waits for them, and re-layouts  2.52 us

profile of v1, /device:TPU:0, one launch (start us, length us, event | category | flops | bytes accessed | tf_op | source)
XLA Modules:
  0.0 93.9 jit_solution(7442798862981028628)
XLA Ops:
  0.6 0.0 copy-start.2
  0.7 0.0 copy-start.3
  0.7 0.7 copy-done.2
  1.3 0.0 copy-done.3
  1.3 0.0 copy-start
  1.3 0.9 %copy-done = bf16[64,2048]{1,0:T(8,128)(2,1)S(1)} copy-done((bf16[64,2048]{1,0:T(8,128)(2,1)S(1)}, bf16[64,2048]{1,0:T(8,128)(2,1)}, u32[]{:S(2)}) %copy-start) | copy-done | bytes 262168
  2.3 0.0 copy-start.1
  2.3 0.9 copy-done.1
  3.2 88.4 %shard_map.67 = (f32[6,128]{1,0:T(8,128)S(1)}, f32[6,128]{1,0:T(8,128)S(1)}, f32[128,384]{1,0:T(8,128)S(1)}, f32[64,2048]{1,0:T(8,128)S(1)}) custom-call(bf16[128,384]{1,0:T(8,128)(2,1)S(1)} %copy-done.1, bf16[64,2048]{1,0:T(8,128)(2,1)S(1)} %copy-done, f32[3,128]{1,0:T(4,128)S(1)} %bitcast.7, f32[2,8,128]{2,1,0:T(8,128)S(1)} %bitcast.4), custom_call_target="tpu_custom_call" | custom-call | flops 2415919104 | bytes 524288 | tf_op jit(solution)/shard_map/pallas_call | solution.py:308
  91.6 0.7 dynamic_slice.6
  92.3 0.1 dynamic_slice.7
  92.3 0.7 multiply_subtract_fusion.1
  93.0 0.9 multiply_subtract_fusion
Async XLA Ops:
  0.6 0.7 copy-start.2
  0.7 0.7 copy-start.3
  1.3 1.0 %copy-start = (bf16[64,2048]{1,0:T(8,128)(2,1)S(1)}, bf16[64,2048]{1,0:T(8,128)(2,1)}, u32[]{:S(2)}) copy-start(bf16[64,2048]{1,0:T(8,128)(2,1)} %y_ref.1) | copy-start | bytes 786436
  2.3 0.9 copy-start.1

commit v2 on v1

v2 whole, which is shorter than its diff:
```python
import functools
import math

import jax
import jax.numpy as jnp
from jax import lax
from jax.experimental import pallas as pl
from jax.experimental.pallas import tpu as pltpu
from jax.sharding import PartitionSpec as P

ITERS = 3


blur = 0.05

LANES = 128
LOG2E = math.log2(math.e)
MESH = pl.DeviceIdType.MESH


def lse2(parts):
    top = jnp.max(parts, 0)
    return top + jnp.log(jnp.sum(jnp.exp2(parts - top[None]), 0)) * LOG2E


def tile_rows(blocks):
    return -(-blocks // 8) * 8


def kernel(
    zn, yn, cn, split, x_ref, y_ref, a_ref, b_ref,
    reward_ref, mass_ref, pulled_ref, xsum_ref,
    xg, yg, neg, pm, plan, fbc, wslots, fslots, gslots, rslots, fv, gv,
    xsend, xmid, xout, xrecv, psend, pmid, pout, precv,
    local_sem, xs, xr, xf, ys, yr, yf, ws, wr, fs, fr, gs, gr, rs, rr,
    us, um, uo, ur, ps, pk, po, pr,
):
    row, col = lax.axis_index("row"), lax.axis_index("col")
    z, y = lax.div(row, yn), lax.rem(row, yn)
    zh, zl = lax.div(z, split), lax.rem(z, split)
    cores = 2 if cn % 2 == 0 else 1
    c = lax.rem(col, cores)
    nrow, ncube, nside = zn * yn, cn * split, (zn // split) * yn
    nchip = ncube // cores
    q = col * split + zl
    chip = lax.div(col, cores) * split + zl
    side = zh * yn + y
    fx, own_rows = x_ref.shape
    fy = y_ref.shape[0]
    width, rows = xg.shape
    cols = yg.shape[1]
    rblocks, cblocks = rows // LANES, cols // LANES
    own_blocks = own_rows // LANES

    def cube_device(index):
        return ((zh * split + lax.rem(index, split)) * yn + y, lax.div(index, split))

    def side_device(index):
        peer = lax.div(index, yn) * split + zl
        return (peer * yn + lax.rem(index, yn), col)

    def cube_index(index, core):
        return (lax.div(index, split) * cores + core) * split + lax.rem(index, split)

    def each(count, body):
        def step(i, carry):
            body(i)
            return carry
        if count > 0:
            lax.fori_loop(0, count, step, 0)

    def others(count, me, body):
        each(count - 1, lambda i: body(lax.rem(me + i + 1, count)))

    def band(index, size):
        return pl.ds(pl.multiple_of(index * size, size), size)

    def remote(src, dst, send, recv, device):
        return pltpu.make_async_remote_copy(
            src_ref=src, dst_ref=dst, send_sem=send, recv_sem=recv,
            device_id=device, device_id_type=MESH)

    wslots[...] = jnp.ones(wslots.shape, jnp.float32)
    wslots[zl, 0:own_blocks, :] = a_ref[...]
    fslots[...] = jnp.zeros(fslots.shape, jnp.float32)
    gslots[...] = jnp.zeros(gslots.shape, jnp.float32)
    rslots[...] = jnp.zeros(rslots.shape, jnp.float32)
    barrier = pltpu.get_barrier_semaphore()
    others(nrow, row, lambda r: pl.semaphore_signal(
        barrier, inc=1, device_id=(r, col), device_id_type=MESH))
    others(ncube, q, lambda p: pl.semaphore_signal(
        barrier, inc=1, device_id=cube_device(p), device_id_type=MESH))
    pl.semaphore_wait(barrier, nrow - 1 + ncube - 1)

    def y_place(origin):
        return yg.at[band(origin, fy), :]

    def y_along(dest, origin):
        return remote(
            y_ref.at[:, band(lax.rem(dest, split), cols)], y_place(origin * yn + y),
            ys.at[dest], yr.at[origin * yn + y], (dest * yn + y, col))

    def y_across(layer, dest, origin):
        place = y_place(layer * yn + origin)
        return remote(
            place, place, yf.at[layer, dest], yr.at[layer * yn + origin], (z * yn + dest, col))

    def y_first(dest):
        return remote(
            y_ref.at[:, band(zl, cols)], y_place(row), yf.at[z, dest], yr.at[row],
            (z * yn + dest, col))

    def x_place(index):
        return xg.at[band(lax.div(index, split), fx), band(lax.rem(index, split), own_rows)]

    def x_copy(dest, origin):
        return remote(x_ref, x_place(origin), xs.at[dest], xr.at[origin], cube_device(dest))

    def x_forward(origin, core):
        return remote(
            x_place(origin), x_place(origin), xf.at[origin, core], xr.at[origin],
            cube_device(cube_index(chip, core)))

    def w_copy(dest, origin):
        return remote(
            wslots.at[origin], wslots.at[origin], ws.at[dest], wr.at[origin],
            ((zh * split + dest) * yn + y, col))

    others(zn, z, lambda p: y_along(p, z).start())
    others(yn, y, lambda p: y_first(p).start())
    others(nchip, chip, lambda p: x_copy(cube_index(p, c), q).start())
    others(cores, c, lambda p: x_copy(cube_index(chip, p), q).start())
    others(split, zl, lambda p: w_copy(p, zl).start())
    own_y = pltpu.make_async_copy(y_ref.at[:, band(zl, cols)], y_place(row), local_sem.at[0])
    own_x = pltpu.make_async_copy(x_ref, x_place(q), local_sem.at[1])
    own_y.start()
    own_x.start()

    def x_relay(p):
        origin = cube_index(p, c)
        x_copy(origin, origin).wait_recv()
        others(cores, c, lambda core: x_forward(origin, core).start())
    others(nchip, chip, x_relay)

    def y_relay(p):
        y_along(p, p).wait_recv()
        others(yn, y, lambda dest: y_across(p, dest, y).start())
    others(zn, z, y_relay)

    log_b = jnp.log(b_ref[zl]) * LOG2E
    own_y.wait()
    own_x.wait()
    others(split, zl, lambda p: w_copy(p, p).wait_recv())
    mass_a = jnp.concatenate([wslots[p, 0:own_blocks, :] for p in range(split)], 0)
    log_a = jnp.log(mass_a) * LOG2E

    def x_rest(core):
        each(nchip, lambda p: x_copy(cube_index(p, core), cube_index(p, core)).wait_recv())
    others(cores, c, x_rest)

    def y_rest(p):
        each(zn, lambda layer: y_across(layer, p, p).wait_recv())
    others(yn, y, y_rest)

    def spread(line):
        return jnp.transpose(jnp.broadcast_to(line, (LANES, LANES)))

    def gather_line(column):
        return jnp.transpose(jnp.broadcast_to(column, (LANES, LANES)))[0:1, :]

    def row_sums(block):
        return jnp.sum(jnp.transpose(block), 0, keepdims=True)

    def part(index):
        return slice(index * LANES, (index + 1) * LANES)

    scale = LOG2E / (blur * width)
    sqy = jnp.zeros((1, cols), jnp.float32)
    for r in range(0, width, LANES):
        some = yg[r:r + LANES, :].astype(jnp.float32)
        sqy = sqy + jnp.sum(some * some, 0, keepdims=True)
    xstep = 2 * LANES if rows % (2 * LANES) == 0 else LANES

    def cost_block(i):
        xb = xg[:, band(i, xstep)]
        xw = xb.astype(jnp.float32)
        sqx = jnp.sum(xw * xw, 0, keepdims=True)
        sqx = jnp.concatenate([spread(sqx[:, part(k)]) for k in range(xstep // LANES)], 0)
        cross = lax.dot_general(
            xb, yg[...], (((0,), (0,)), ((), ())), preferred_element_type=jnp.float32)
        neg[band(i, xstep), :] = (2.0 * cross - (sqx[:, 0:1] + sqy)) * scale
    each(rows // xstep, cost_block)

    def exchange(slots, count, me, sends, recvs, device):
        def copy(dest, origin):
            return remote(
                slots.at[origin], slots.at[origin], sends.at[dest], recvs.at[origin],
                device(dest))
        others(count, me, lambda p: copy(p, me).start())

        def arrive():
            others(count, me, lambda p: copy(p, p).wait_recv())

        def leave():
            others(count, me, lambda p: copy(p, me).wait_send())
        return arrive, leave

    leaves = []

    def over_cube(t):
        arrive, leave = exchange(fslots.at[t], ncube, q, fs.at[t], fr.at[t], cube_device)
        leaves.append(leave)
        arrive()
        return fslots[t, :, 0:rblocks, :]

    def over_side(t):
        arrive, leave = exchange(gslots.at[t], nside, side, gs.at[t], gr.at[t], side_device)
        leaves.append(leave)
        arrive()
        return gslots[t, :, 0:cblocks, :]

    def set_rows(value):
        fv[0:rblocks, :] = value
        for i in range(rblocks):
            fbc[part(i), :] = spread(fv[i:i + 1, :])

    def first_rows(i):
        here = band(i, LANES)
        high = neg[here, part(0)]
        for k in range(1, cblocks):
            high = jnp.maximum(high, neg[here, part(k)])
        top = jnp.max(high, 1, keepdims=True)
        total = jnp.exp2(neg[here, part(0)] - top)
        for k in range(1, cblocks):
            total = total + jnp.exp2(neg[here, part(k)] - top)
        line = top + jnp.log(jnp.sum(total, 1, keepdims=True)) * LOG2E
        fslots[0, q, pl.ds(i, 1), :] = gather_line(line)
    each(rblocks, first_rows)
    set_rows(log_a - lse2(over_cube(0)))

    def first_cols(k):
        here = band(k, LANES)

        def score(i):
            return neg[part(i), here] + fbc[part(i), :]

        high = score(0)
        for i in range(1, rblocks):
            high = jnp.maximum(high, score(i))
        top = jnp.max(high, 0, keepdims=True)
        total = jnp.exp2(score(0) - top)
        for i in range(1, rblocks):
            total = total + jnp.exp2(score(i) - top)
        line = top + jnp.log(jnp.sum(total, 0, keepdims=True)) * LOG2E
        gslots[0, side, pl.ds(k, 1), :] = line
    each(cblocks, first_cols)
    gv[0:cblocks, :] = log_b - lse2(over_side(0))
    mass_b = b_ref[zl]

    for t in range(1, ITERS):
        for i in range(rblocks):
            total = jnp.zeros((LANES, LANES), jnp.float32)
            for k in range(cblocks):
                if t == 1:
                    value = jnp.exp2(neg[part(i), part(k)] + fbc[part(i), :] + gv[k:k + 1, :])
                    pm[part(i), part(k)] = value
                    total = total + value
                else:
                    total = total + pm[part(i), part(k)] * gv[k:k + 1, :]
            fslots[t, q, i:i + 1, :] = row_sums(total)
        set_rows(mass_a / jnp.sum(over_cube(t), 0))
        for k in range(cblocks):
            total = pm[part(0), part(k)] * fbc[part(0), :]
            for i in range(1, rblocks):
                total = total + pm[part(i), part(k)] * fbc[part(i), :]
            gslots[t, side, k:k + 1, :] = jnp.sum(total, 0, keepdims=True)
        gv[0:cblocks, :] = mass_b / jnp.sum(over_side(t), 0)

    for i in range(rblocks):
        for k in range(cblocks):
            value = pm[part(i), part(k)] * fbc[part(i), :] * gv[k:k + 1, :]
            plan[part(i), part(k)] = value.astype(jnp.bfloat16)

    step = 2 * LANES if cols % (2 * LANES) == 0 else LANES

    def xsum_block(k):
        here = band(k, step)
        xsend[:, here] = jnp.dot(
            xg[...], plan[:, here], preferred_element_type=jnp.float32).astype(jnp.bfloat16)
    each(cols // step, xsum_block)

    def u_across(layer, dest, origin):
        return remote(
            xsend.at[band(layer * yn + dest, fy), :], xmid.at[layer, origin],
            us.at[layer, dest], um.at[layer, origin], (z * yn + dest, col))

    def u_along(dest, origin):
        return remote(
            xout.at[dest], xrecv.at[origin], uo.at[dest], ur.at[origin], (dest * yn + y, col))

    def u_start(layer):
        others(yn, y, lambda dest: u_across(layer, dest, y).start())
    others(zn, z, u_start)
    u_start(z)

    rstep = 2 * LANES if rows % (2 * LANES) == 0 else LANES

    def pull_block(i):
        here = band(i, rstep)
        psend[:, here] = lax.dot_general(
            yg[...], plan[here, :], (((1,), (1,)), ((), ())),
            preferred_element_type=jnp.float32).astype(jnp.bfloat16)
    each(rows // rstep, pull_block)

    def p_place(index):
        return band(lax.div(index, split), fx), band(lax.rem(index, split), own_rows)

    def p_across(index, dest, origin):
        return remote(
            psend.at[p_place(cube_index(index, dest))], pmid.at[index, origin],
            ps.at[index, dest], pk.at[index, origin], cube_device(cube_index(chip, dest)))

    def p_along(dest, origin):
        return remote(
            pout.at[dest], precv.at[origin], po.at[dest], pr.at[origin],
            cube_device(cube_index(dest, c)))

    def p_start(index):
        others(cores, c, lambda dest: p_across(index, dest, c).start())
    others(nchip, chip, p_start)
    p_start(chip)

    def u_total(layer):
        own = xsend[band(layer * yn + y, fy), :].astype(jnp.float32)
        for d in range(1, yn):
            origin = lax.rem(y + d, yn)
            u_across(layer, origin, origin).wait_recv()
            own = own + xmid[layer, origin].astype(jnp.float32)
        return own.astype(jnp.bfloat16)

    def p_total(index):
        own = psend[p_place(cube_index(index, c))].astype(jnp.float32)
        for d in range(1, cores):
            origin = lax.rem(c + d, cores)
            p_across(index, origin, origin).wait_recv()
            own = own + pmid[index, origin].astype(jnp.float32)
        return own.astype(jnp.bfloat16)

    def u_pass(layer):
        xout[layer] = u_total(layer)
        u_along(layer, z).start()

    def p_pass(index):
        pout[index] = p_total(index)
        p_along(index, chip).start()

    others(nchip, chip, p_pass)
    others(zn, z, u_pass)
    precv[chip] = p_total(chip)

    half = rslots.shape[1] // 2
    for i in range(rblocks):
        total = jnp.zeros((LANES, LANES), jnp.float32)
        moment = jnp.zeros((LANES, LANES), jnp.float32)
        for k in range(cblocks):
            weight = pm[part(i), part(k)] * gv[k:k + 1, :]
            total = total + weight
            moment = moment + weight * neg[part(i), part(k)]
        rslots[q, i:i + 1, :] = row_sums(total)
        rslots[q, half + i:half + i + 1, :] = row_sums(moment)
    arrive, leave = exchange(rslots, ncube, q, rs, rr, cube_device)
    leaves.append(leave)
    xrecv[z] = u_total(z)
    arrive()
    total = jnp.sum(rslots[:, 0:rblocks, :], 0)
    moment = jnp.sum(rslots[:, half:half + rblocks, :], 0)
    reward_ref[...] = moment / total * (blur / LOG2E)
    mass_ref[...] = fv[0:rblocks, :] * total

    others(nchip, chip, lambda p: p_along(p, p).wait_recv())
    summed = precv[0].astype(jnp.float32)
    for p in range(1, nchip):
        summed = summed + precv[p].astype(jnp.float32)
    pulled_ref[...] = summed
    others(zn, z, lambda p: u_along(p, p).wait_recv())
    for p in range(split):
        summed = xrecv[p].astype(jnp.float32)
        for s in range(1, zn // split):
            summed = summed + xrecv[s * split + p].astype(jnp.float32)
        xsum_ref[:, p * cols:(p + 1) * cols] = summed

    others(zn, z, lambda p: y_along(p, z).wait_send())
    others(yn, y, lambda p: y_first(p).wait_send())
    others(zn, z, lambda layer: others(
        yn, y, lambda dest: y_across(layer, dest, y).wait_send()))
    others(nchip, chip, lambda p: x_copy(cube_index(p, c), q).wait_send())
    others(cores, c, lambda p: x_copy(cube_index(chip, p), q).wait_send())
    others(nchip, chip, lambda p: others(
        cores, c, lambda core: x_forward(cube_index(p, c), core).wait_send()))
    others(split, zl, lambda p: w_copy(p, zl).wait_send())
    for leave in leaves:
        leave()
    each(zn, lambda layer: others(
        yn, y, lambda dest: u_across(layer, dest, y).wait_send()))
    others(zn, z, lambda p: u_along(p, z).wait_send())
    each(nchip, lambda p: others(
        cores, c, lambda dest: p_across(p, dest, c).wait_send()))
    others(nchip, chip, lambda p: p_along(p, chip).wait_send())


def shards(zn, yn, cn, split, roll_embed, expert_embed, roll_weight, expert_weight):
    fx, own_rows = roll_embed.shape
    fy, own_cols = expert_embed.shape
    width = fx * cn
    rows, cols = own_rows * split, own_cols // split
    rblocks, cblocks = rows // LANES, cols // LANES
    nrow, ncube, nside = zn * yn, cn * split, (zn // split) * yn
    cores = 2 if cn % 2 == 0 else 1
    nchip = ncube // cores
    f32, bf16 = jnp.float32, jnp.bfloat16
    dma = pltpu.SemaphoreType.DMA
    rt, ct, wt = tile_rows(rblocks), tile_rows(cblocks), tile_rows(own_rows // LANES)
    vmem = pl.BlockSpec(memory_space=pltpu.VMEM)
    reward, mass, pulled, xsum = pl.pallas_call(
        functools.partial(kernel, zn, yn, cn, split),
        out_shape=(
            jax.ShapeDtypeStruct((rblocks, LANES), f32),
            jax.ShapeDtypeStruct((rblocks, LANES), f32),
            jax.ShapeDtypeStruct((fx, own_rows), f32),
            jax.ShapeDtypeStruct((fy, own_cols), f32),
        ),
        in_specs=[vmem] * 4,
        out_specs=[vmem] * 4,
        scratch_shapes=[
            pltpu.VMEM((width, rows), bf16),
            pltpu.VMEM((width, cols), bf16),
            pltpu.VMEM((rows, cols), f32),
            pltpu.VMEM((rows, cols), f32),
            pltpu.VMEM((rows, cols), bf16),
            pltpu.VMEM((rows, LANES), f32),
            pltpu.VMEM((split, wt, LANES), f32),
            pltpu.VMEM((ITERS, ncube, rt, LANES), f32),
            pltpu.VMEM((ITERS, nside, ct, LANES), f32),
            pltpu.VMEM((ncube, 2 * rt, LANES), f32),
            pltpu.VMEM((rt, LANES), f32),
            pltpu.VMEM((ct, LANES), f32),
            pltpu.VMEM((width, cols), bf16),
            pltpu.VMEM((zn, yn, fy, cols), bf16),
            pltpu.VMEM((zn, fy, cols), bf16),
            pltpu.VMEM((zn, fy, cols), bf16),
            pltpu.VMEM((width, rows), bf16),
            pltpu.VMEM((nchip, cores, fx, own_rows), bf16),
            pltpu.VMEM((nchip, fx, own_rows), bf16),
            pltpu.VMEM((nchip, fx, own_rows), bf16),
            dma((2,)),
            dma((ncube,)), dma((ncube,)), dma((ncube, cores)),
            dma((zn,)), dma((nrow,)), dma((zn, yn)),
            dma((split,)), dma((split,)),
            dma((ITERS, ncube)), dma((ITERS, ncube)),
            dma((ITERS, nside)), dma((ITERS, nside)),
            dma((ncube,)), dma((ncube,)),
            dma((zn, yn)), dma((zn, yn)), dma((zn,)), dma((zn,)),
            dma((nchip, cores)), dma((nchip, cores)), dma((nchip,)), dma((nchip,)),
        ],
        compiler_params=pltpu.CompilerParams(
            collective_id=0, has_side_effects=True, vmem_limit_bytes=48 * 2**20),
        cost_estimate=pl.CostEstimate(
            flops=6 * rows * cols * width, bytes_accessed=4 * fy * own_cols,
            transcendentals=3 * rows * cols),
    )(
        roll_embed, expert_embed,
        roll_weight.reshape(own_rows // LANES, LANES),
        expert_weight.reshape(split, cblocks, LANES),
    )
    start = lax.rem(lax.div(lax.axis_index("row"), yn), split) * own_rows
    reward = lax.dynamic_slice_in_dim(reward.reshape(rows), start, own_rows, 0)
    mass = lax.dynamic_slice_in_dim(mass.reshape(rows), start, own_rows, 0)
    roll_pull = mass[None, :] * roll_embed.astype(f32) - pulled
    expert_pull = expert_weight[None, :] * expert_embed.astype(f32) - xsum
    return (reward, roll_pull, expert_pull)


def solution(mesh):
    cn = mesh.shape["col"]
    yn = max(cn // 2, 1)
    if mesh.shape["row"] % yn:
        yn = 1
    zn = mesh.shape["row"] // yn
    split = 2 if zn % 2 == 0 else 1
    placed = (P("col", "row"), P("row", "col"), P("row"), P("col"))
    return jax.shard_map(
        functools.partial(shards, zn, yn, cn, split),
        mesh=mesh,
        in_specs=placed,
        out_specs=(P("row"), P("col", "row"), P("row", "col")),
        check_vma=False,
    )
```

time: 94.1 us -> 84.8 us (0.901)
  Pallas kernels: 88.4 us -> 79.1 us
    pallas_call x1, Pallas kernels: 88.4 us -> 79.1 us  [shards(): pl.pallas_call(functools.partial(kernel, zn, yn, cn, split), out_shape=(j...]
where the time goes in v2:
time: 84.8 us; the launch traced here: 84.6 us
  Pallas kernels  79.1 us (93%)
  local copies, waits for them, and re-layouts  3.25 us (4%)
  other arithmetic  1.57 us (2%)
    pallas_call x1, Pallas kernels, shards(): pl.pallas_call(functools.partial(kernel, zn, yn, cn, split), out_shape=(j...  79.1 us
    unnamed x8, local copies, waits for them, and re-layouts  2.52 us

profile of v2, /device:TPU:0, one launch (start us, length us, event | category | flops | bytes accessed | tf_op | source)
XLA Modules:
  0.0 84.6 jit_solution(8416047647725764121)
XLA Ops:
  0.6 0.0 copy-start.2
  0.7 0.0 copy-start.3
  0.7 0.7 copy-done.2
  1.3 0.0 copy-done.3
  1.3 0.0 copy-start
  1.3 0.9 %copy-done = bf16[64,2048]{1,0:T(8,128)(2,1)S(1)} copy-done((bf16[64,2048]{1,0:T(8,128)(2,1)S(1)}, bf16[64,2048]{1,0:T(8,128)(2,1)}, u32[]{:S(2)}) %copy-start) | copy-done | bytes 262168
  2.3 0.0 copy-start.1
  2.3 0.9 %copy-done.1 = bf16[128,384]{1,0:T(8,128)(2,1)S(1)} copy-done((bf16[128,384]{1,0:T(8,128)(2,1)S(1)}, bf16[128,384]{1,0:T(8,128)(2,1)}, u32[]{:S(2)}) %copy-start.1) | copy-done | bytes 98328
  3.2 79.1 %shard_map.67 = (f32[6,128]{1,0:T(8,128)S(1)}, f32[6,128]{1,0:T(8,128)S(1)}, f32[128,384]{1,0:T(8,128)S(1)}, f32[64,2048]{1,0:T(8,128)S(1)}) custom-call(bf16[128,384]{1,0:T(8,128)(2,1)S(1)} %copy-done.1, bf16[64,2048]{1,0:T(8,128)(2,1)S(1)} %copy-done, f32[3,128]{1,0:T(4,128)S(1)} %bitcast.7, f32[2,8,128]{2,1,0:T(8,128)S(1)} %bitcast.4), custom_call_target="tpu_custom_call" | custom-call | flops 2415919104 | bytes 524288 | tf_op jit(solution)/shard_map/pallas_call | solution.py:424
  82.3 0.7 dynamic_slice.6
  83.0 0.1 dynamic_slice.7
  83.1 0.7 multiply_subtract_fusion.1
  83.8 0.9 %multiply_subtract_fusion = f32[64,2048]{1,0:T(8,128)} fusion(f32[64,2048]{1,0:T(8,128)S(1)} %get-tuple-element.10, bf16[64,2048]{1,0:T(8,128)(2,1)S(1)} %copy-done, f32[2048]{0:T(1024)S(1)} %copy-done.2), kind=kLoop, calls=%fused_computation | loop fusion | flops 393216 | bytes 1318912 | tf_op jit(solution)/shard_map/sub | solution.py:479
Async XLA Ops:
  0.6 0.7 copy-start.2
  0.7 0.7 copy-start.3
  1.3 0.9 %copy-start = (bf16[64,2048]{1,0:T(8,128)(2,1)S(1)}, bf16[64,2048]{1,0:T(8,128)(2,1)}, u32[]{:S(2)}) copy-start(bf16[64,2048]{1,0:T(8,128)(2,1)} %y_ref.1) | copy-start | bytes 786436
  2.3 0.9 %copy-start.1 = (bf16[128,384]{1,0:T(8,128)(2,1)S(1)}, bf16[128,384]{1,0:T(8,128)(2,1)}, u32[]{:S(2)}) copy-start(bf16[128,384]{1,0:T(8,128)(2,1)} %x_ref.1) | copy-start | bytes 294916
